TPU v7x, 32 devices: a whole 2x2x4 slice. The times are simulated.
32 devices in a mesh: cfg: 2 (over core), req: 16 (over z, y, x).
Axes of the slice: x: 2, y: 2, z: 4, core: 2. Of those that a mesh axis runs over, the one named last changes fastest.
Arguments:
- query_rows: bfloat16 [2, 8192, 2560], P('cfg', 'req'), may hold values from -32 to 32
- key_rows: bfloat16 [2, 8192, 2560], P('cfg', 'req'), may hold values from -6 to 6
- value_rows: bfloat16 [2, 8192, 2560], P('cfg', 'req'), may hold values from -600 to 600
- positions: int32 [3, 8192], P(None, 'req'), may hold values from 0 to 51
- latents: float32 [8192, 64], P('req', 'cfg'), may hold values from -6 to 6
- w_head: bfloat16 [2560, 64], replicated, may hold values from -0.125 to 0.125
- modulation: float32 [2, 2560], replicated, may hold values from -0.5 to 1
- guide_scale: float32 [1], replicated, may hold values from 4 to 6
- step_sizes: float32 [32], replicated, may hold values from -0.4 to -0.1
- lengths: int32 [32], replicated, may hold values from 1 to 512, 8192 in all
Outputs:
- next_latents: float32 [8192, 64], P('req', 'cfg')
Inputs may be any that keep to these rules, and one draw needn't show every extreme that they name: Videos are laid end to end in the given order and their lengths sum to 8192.
All inputs are finite; a program needn't handle non-finite values.
Results may differ from a plain program's by a relative error of at most 0.0059.
Values may be sent and summed in bfloat16 or wider, within the bound.
No kernel may reach another device: no remote copies, remote signals or barrier semaphores. Data moves between devices by JAX's collectives and lax.ppermute only.
A program may use at most 128 MiB of HBM per device.

v0:
```python
import functools
import math

import jax
import jax.numpy as jnp
import numpy
from jax import lax
from jax.experimental import pallas as pl
from jax.experimental.pallas import tpu as pltpu
from jax.sharding import PartitionSpec as P

HD = 128
TILE = 16
BLK = 128
CHUNKS = 4
MORE = 48
EXTRA = 16
EARLY_CHUNKS = 2
rope_theta = 10000.0
NEG = -1e30
SCALE2 = math.log2(math.e) / math.sqrt(HD)

PASS, DIRECT = 0, 16
LB, RB, LROWS, RROWS, HEAD0, KEEP, EARLY, SOURCE = range(8)
OWN_FROM, OWN_TO, OWN, FAR_TO, FAR, SIDE = range(8, 14)
SEND = 32
ROW, TILES, FIRST, HEADS = range(4)
MOST, INNER_FROM, INNER_TO = 40, 41, 42
SCALARS = 48
MIB = 1024 * 1024


def sizes(rows, heads):
    tiles = rows // TILE
    cap = max(
        min(max(a * n, (tiles + 1 - a) * (heads - n)) for n in range(heads + 1))
        for a in range(1, tiles + 1)
    )
    padded = -(-cap // TILE) * TILE
    return cap, padded, 2 * padded


def angles(positions):
    pair_total = HD // 2
    side_pairs = HD // 6
    time_pairs = pair_total - 2 * side_pairs
    column = jnp.arange(HD, dtype=jnp.int32) // 2
    in_time = column < time_pairs
    in_height = (column >= time_pairs) & (column < time_pairs + side_pairs)
    in_width = column >= time_pairs + side_pairs
    local_index = jnp.where(
        in_time, column, jnp.where(in_height, column - time_pairs, column - time_pairs - side_pairs)
    )
    axis_pairs = jnp.where(in_time, time_pairs, side_pairs)
    frequency = jnp.exp(
        -(local_index.astype(jnp.float32) / axis_pairs.astype(jnp.float32)) * math.log(rope_theta)
    )
    selector = jnp.stack([in_time, in_height, in_width]).astype(jnp.float32) * frequency[None, :]
    placed = positions.astype(jnp.float32)
    return (
        placed[0][:, None] * selector[0][None, :]
        + placed[1][:, None] * selector[1][None, :]
        + placed[2][:, None] * selector[2][None, :]
    )


def plan_kernel(rows, heads, count, lengths, out, ls, rs, split, least):
    cap, padded, _ = sizes(rows, heads)
    here = lax.axis_index("req")
    shift = rows.bit_length() - 1

    def clear(b, carry):
        ls[b] = 0
        rs[b] = 0
        return carry

    lax.fori_loop(0, count + 8, clear, 0)

    def one_video(v, start):
        end = start + lengths[v]
        b = lax.shift_right_logical(end - 1, shift) if rows == 1 << shift else lax.div(end - 1, rows)
        at = b * rows

        @pl.when(start < at)
        def _():
            ls[b] = at - start
            rs[b] = end - at

        return end

    lax.fori_loop(0, lengths.shape[0], one_video, 0)
    budget = 3.0 * lax.broadcasted_iota(jnp.int32, (8, 128), 1).astype(jnp.float32)
    split[...] = jnp.zeros_like(split)

    def tiles_of(x):
        return lax.shift_right_logical(x + TILE - 1, 4)

    def eight(b):
        return pl.ds(pl.multiple_of(b * 8, 8), 8)

    def per_tile(x, tiles):
        return jnp.floor((x + 0.5) * (1.0 / jnp.maximum(tiles, 1.0)))

    def facts(b):
        direct = lax.rem(b, 2).astype(jnp.float32)
        lt, rt = (jnp.full((8, 128), tiles_of(x[b]).astype(jnp.float32)) for x in (ls, rs))
        return lt, rt, padded + direct * 1e6

    def five_at_a_time(step, carry):
        def body(i, carry):
            for u in range(5):
                carry = step(5 * i + u, carry)
            return carry

        return lax.fori_loop(0, -(-(count - 1) // 5), body, carry)

    def from_right(i, load):
        b = -(-(count - 1) // 5) * 5 - i
        lt, rt, limit = facts(b)
        room = jnp.minimum(budget - load, limit)
        n = jnp.where(rt > 0.0, jnp.maximum(heads - per_tile(room, rt), 0.0), 0.0)
        least[eight(b)] = jnp.where(room >= 0.0, n, 1e6)
        return lt * n

    def from_left(i, carry):
        load, ok = carry
        b = i + 1
        lt, rt, limit = facts(b)
        room = jnp.minimum(budget - load, limit)
        most = jnp.where(lt > 0.0, jnp.minimum(per_tile(room, lt), float(heads)), 0.0)
        low = least[eight(b)]
        even = jnp.floor(heads * rt / jnp.maximum(lt + rt, 1.0) + 0.5)
        n = jnp.minimum(most, jnp.maximum(low, even))
        split[eight(b)] = n
        return rt * (heads - n), jnp.where((room >= 0.0) & (low <= most), ok, 0.0)

    zero = jnp.zeros((8, 128), jnp.float32)
    five_at_a_time(from_right, zero)
    load, ok = five_at_a_time(from_left, (zero, zero + 1.0))
    ok = jnp.where(load <= budget, ok, 0.0)
    most = jnp.min(jnp.where((ok > 0.0) & (budget >= (padded + MORE) // 3 * 3), budget, 1e9))
    out[MOST] = most.astype(jnp.int32)

    def head_split(b):
        n = split[eight(b)]
        return jnp.max(jnp.where(budget == most, n, 0.0)).astype(jnp.int32)

    even = lax.rem(here, 2) == 0
    beyond = jnp.where(even, here + 2, here - 1)
    n_left, n_right, n_beyond = head_split(here), head_split(here + 1), head_split(beyond)
    partner_passes = jnp.where(
        even,
        tiles_of(ls[beyond]) * n_beyond,
        tiles_of(rs[beyond]) * (heads - n_beyond),
    )
    for side, b, n in ((0, here, n_left), (1, here + 1, n_right)):
        direct = jnp.logical_not(even) if side == 0 else even
        at = jnp.where(direct, DIRECT, PASS)
        lt, rt = tiles_of(ls[b]), tiles_of(rs[b])
        none = jnp.where(lt > 0, 0, heads)
        keep = n if side == 0 else jnp.maximum(heads - n - none, 0)
        far = lt if side == 0 else rt
        out[at + LB], out[at + RB] = lt, rt
        out[at + LROWS], out[at + RROWS] = ls[b], rs[b]
        out[at + HEAD0] = 0 if side == 0 else n
        out[at + KEEP] = keep
        source = jnp.where(direct, partner_passes, 0)
        there = jnp.where(direct, padded + MORE, padded // CHUNKS * EARLY_CHUNKS) - source
        out[at + EARLY] = jnp.minimum(keep, lax.div(jnp.maximum(there, 0), jnp.maximum(far, 1)))
        out[at + SOURCE] = source
        out[at + OWN_FROM] = 0 if side == 0 else rows // TILE - lt
        out[at + OWN_TO] = lt if side == 0 else 0
        out[at + OWN] = rt if side == 0 else lt
        out[at + FAR_TO] = 0 if side == 0 else lt
        out[at + FAR] = far
        out[at + SIDE] = side
        to = SEND + jnp.where(direct, 4, 0)
        out[to + ROW] = 0 if side == 0 else rows - TILE * lt
        out[to + TILES] = rt if side == 0 else lt
        out[to + FIRST] = n if side == 0 else 0
        out[to + HEADS] = jnp.maximum(heads - n - none, 0) if side == 0 else n
    out[INNER_FROM] = rs[here]
    out[INNER_TO] = rows - ls[here + 1]


def in_groups(low, high, step):
    count = high - low

    def run(group, times):
        def body(i, carry):
            step(jnp.minimum(low + group * i, high - group), group)
            return carry

        lax.fori_loop(0, times, body, 0)

    run(8, jnp.where(count >= 8, lax.shift_right_logical(count + 7, 3), 0))
    run(2, jnp.where((count >= 2) & (count < 8), lax.shift_right_logical(count + 1, 1), 0))
    run(1, jnp.where(count == 1, 1, 0))


def lanes_of(h):
    return pl.ds(pl.multiple_of(h * HD, HD), HD)


def rows_of(t, group):
    return pl.ds(pl.multiple_of(t * TILE, TILE), group * TILE)


def turn(x, cosine, sine):
    wide = x.astype(jnp.float32)
    even = lax.rem(lax.broadcasted_iota(jnp.int32, wide.shape, 1), 2) == 0
    swapped = jnp.where(even, pltpu.roll(wide, HD - 1, 1), pltpu.roll(wide, 1, 1))
    return (wide * cosine + swapped * sine).astype(jnp.bfloat16)


def pack(scal, low, high, box, heads, get):
    base = 0
    for what in (SEND, SEND + 4):
        first_tile = lax.shift_right_logical(scal[what + ROW], 4)
        tiles, first, count = scal[what + TILES], scal[what + FIRST], scal[what + HEADS]

        def one_head(i, carry):
            start = base + (pl.program_id(0) * heads + i - first) * tiles
            begin = jnp.clip(low - start, 0, tiles)
            end = jnp.clip(high - start, 0, tiles)
            lanes = lanes_of(i)

            def step(t, group):
                q, k, v = get(rows_of(first_tile + t, group), lanes)
                item = pl.ds(start + t - low, group)
                box[item, 0:TILE] = q.reshape(group, TILE, HD)
                box[item, TILE : 2 * TILE] = k.reshape(group, TILE, HD)
                box[item, 2 * TILE : 3 * TILE] = v.reshape(group, TILE, HD)

            in_groups(begin, end, step)
            return carry

        before = first - pl.program_id(0) * heads
        lax.fori_loop(
            jnp.clip(before, 0, heads), jnp.clip(before + count, 0, heads), one_head, 0
        )
        base = base + tiles * count


def send_off(box, outs, sems):
    @pl.when(pl.program_id(0) == pl.num_programs(0) - 1)
    def _():
        at, copies = 0, []
        for i, out in enumerate(outs):
            copies.append(pltpu.make_async_copy(box.at[pl.ds(at, out.shape[0])], out, sems.at[i]))
            at += out.shape[0]
        for copy in copies:
            copy.start()
        for copy in copies:
            copy.wait()


def first_kernel(scal, q_hbm, k_hbm, v_hbm, cos_ref, sin_ref, box, qs, ks, vs, sems):
    limit = box.shape[0]
    ahead = qs.shape[0] - 1

    def heads_in(what, base):
        tiles = jnp.maximum(scal[what + TILES], 1)
        taken = lax.div(jnp.maximum(limit - base, 0) + tiles - 1, tiles)
        return jnp.minimum(scal[what + HEADS], taken)

    passed = scal[SEND + TILES] * scal[SEND + HEADS]
    count_pass = heads_in(SEND, 0)
    count = count_pass + heads_in(SEND + 4, passed)

    def entry(w):
        direct = w >= count_pass
        what = jnp.where(direct, SEND + 4, SEND)
        slot = w - jnp.where(direct, count_pass, 0)
        tiles = scal[what + TILES]
        start = jnp.where(direct, passed, 0) + slot * tiles
        return scal[what + FIRST] + slot, scal[what + ROW], tiles, start

    rows = cos_ref.shape[0]

    def each_copy(w, act):
        at = lax.rem(w, ahead + 1)
        head, row, tiles, _ = entry(w)
        few = tiles * TILE <= BLK
        block = pl.ds(pl.multiple_of(jnp.minimum(row, rows - BLK), TILE), BLK)
        for need, some in ((few, block), (jnp.logical_not(few), pl.ds(0, rows))):

            @pl.when(need)
            def _(some=some):
                for x, (source, place) in enumerate(((q_hbm, qs), (k_hbm, ks), (v_hbm, vs))):
                    act(pltpu.make_async_copy(
                        source.at[some, lanes_of(head)], place.at[at, some, :], sems.at[at, x]
                    ))

    for w in range(ahead):

        @pl.when(w < count)
        def _(w=w):
            each_copy(w, lambda copy: copy.start())

    def one_head(w, carry):
        @pl.when(w + ahead < count)
        def _():
            each_copy(w + ahead, lambda copy: copy.start())

        each_copy(w, lambda copy: copy.wait())
        at = lax.rem(w, ahead + 1)
        _, row, tiles, start = entry(w)
        first_tile = lax.shift_right_logical(row, 4)

        def step(t, group):
            source = rows_of(first_tile + t, group)
            cosine, sine = cos_ref[source, :], sin_ref[source, :]
            item = pl.ds(start + t, group)
            q, k = turn(qs[at, source, :], cosine, sine), turn(ks[at, source, :], cosine, sine)
            box[item, 0:TILE] = q.reshape(group, TILE, HD)
            box[item, TILE : 2 * TILE] = k.reshape(group, TILE, HD)
            box[item, 2 * TILE : 3 * TILE] = vs[at, source, :].reshape(group, TILE, HD)

        in_groups(0, jnp.clip(limit - start, 0, tiles), step)
        return carry

    lax.fori_loop(0, count, one_head, 0)


def second_kernel(
    low, scal, q_ref, k_ref, v_ref, cos_ref, sin_ref, swap_ref, wt_ref, mod_ref, qr_ref, kr_ref, w_ref, shift_ref, *rest
):
    outs, box, sems = rest[:-3], rest[-2], rest[-1]
    rows = q_ref.shape[0]
    heads = q_ref.shape[1] // HD
    wide = swap_ref.shape[0]

    @pl.when(pl.program_id(0) == 0)
    def _():
        w = wt_ref[...].astype(jnp.float32)
        scaled = w * (1.0 + mod_ref[1:2, :])
        high = scaled.astype(jnp.bfloat16)
        low = (scaled - high.astype(jnp.float32)).astype(jnp.bfloat16)
        w_ref[...] = jnp.concatenate([high, low], axis=0)
        shift = jnp.sum(w * mod_ref[0:1, :], axis=1, keepdims=True)
        shift_ref[...] = jnp.broadcast_to(shift, shift_ref.shape)

    for source, to in ((q_ref, qr_ref), (k_ref, kr_ref)):
        for h in range(0, heads, wide // HD):
            for j in range(rows // BLK):
                at = slice(j * BLK, (j + 1) * BLK)
                x = source[at, h * HD : h * HD + wide]
                swapped = jnp.dot(x, swap_ref[: x.shape[1], : x.shape[1]], preferred_element_type=jnp.float32)
                for i in range(x.shape[1] // HD):
                    lanes = slice(i * HD, (i + 1) * HD)
                    to[at, (h + i) * HD : (h + i + 1) * HD] = (
                        x[:, lanes].astype(jnp.float32) * cos_ref[at, :] + swapped[:, lanes] * sin_ref[at, :]
                    ).astype(jnp.bfloat16)

    def get(rows, lanes):
        return qr_ref[rows, lanes], kr_ref[rows, lanes], v_ref[rows, lanes]

    pack(scal, low, low + box.shape[0], box, heads, get)
    send_off(box, outs, sems)


def dot_t(a, b):
    return lax.dot_general(a, b, (((1,), (1,)), ((), ())), preferred_element_type=jnp.float32)


def attend_rows(q, k, v_ones, masked):
    s = masked(dot_t(q, k))
    top = jnp.max(s, axis=1, keepdims=True)
    weight = jnp.exp2(s * SCALE2 - top * SCALE2).astype(jnp.bfloat16)
    both = jnp.dot(weight, v_ones, preferred_element_type=jnp.float32)
    return (both[:, :HD] / both[:, HD:]).astype(jnp.bfloat16)


def projected(o_ref, w_ref, out_ref, rows):
    for j in range(rows // BLK):
        at = slice(j * BLK, (j + 1) * BLK)
        z = dot_t(o_ref[at, :], w_ref[...])
        z = z + pltpu.roll(z, HD // 2, 1)
        lane = lax.broadcasted_iota(jnp.int32, z.shape, 1)
        squares = jnp.zeros(z.shape, jnp.float32)
        for h in range(o_ref.shape[1] // HD):
            wide = o_ref[at, h * HD : (h + 1) * HD].astype(jnp.float32)
            squares = squares + wide * wide
        total = jnp.sum(squares, axis=1, keepdims=True)
        out_ref[at, :] = jnp.where(lane < HD // 2, z, jnp.where(lane == HD // 2, total, 0.0))


def inner_kernel(scal, q_ref, k_ref, v_ref, w_ref, qv_ref, kv_ref, out_ref, o_ref):
    g = pl.program_id(0)
    rows, width = q_ref.shape
    ones = jnp.ones((rows, HD), jnp.bfloat16)
    for j in range(rows // BLK):
        at = pl.ds(j * BLK, BLK)
        same = qv_ref[at, :] == kv_ref[...]
        for i in range(width // HD):
            lanes = slice(i * HD, (i + 1) * HD)
            v_ones = jnp.concatenate([v_ref[:, lanes], ones], axis=1)
            o_ref[at, pl.ds(pl.multiple_of(g * width + i * HD, HD), HD)] = attend_rows(
                q_ref[at, lanes], k_ref[:, lanes], v_ones, lambda s: jnp.where(same, s, NEG)
            )

    @pl.when(g == pl.num_programs(0) - 1)
    def _():
        projected(o_ref, w_ref, out_ref, rows)


def across(scal, at, offset, low, high, sources, items, w_ref, own_sems, places, o_ref, zz):
    rows = zz.shape[0] // 2
    left, right = scal[at + LB], scal[at + RB]
    lead = left * TILE - scal[at + LROWS]
    end = left * TILE + scal[at + RROWS]
    blocks = jnp.minimum(lax.div((left + right) * TILE + BLK - 1, BLK), rows // BLK)
    own_at = jnp.where(scal[at + SIDE] == 0, rows, 0) + left * TILE
    pairs = lax.shift_right_logical(high - low + 1, 1)

    def heads_of(i):
        return [jnp.minimum(low + 2 * i + u, high - 1) for u in range(2)]

    def own_copies(i, act):
        slot = lax.rem(i, 2)
        few = scal[at + OWN] * TILE <= rows // 2
        begin = jnp.where(scal[at + SIDE] == 0, 0, rows // 2)
        for need, begin, size in ((few, begin, rows // 2), (jnp.logical_not(few), 0, rows)):

            @pl.when(need)
            def _(begin=begin, size=size):
                source_rows = pl.ds(pl.multiple_of(begin, TILE), size)
                to = pl.ds(pl.multiple_of(own_at + begin, TILE), size)
                for u, s in enumerate(heads_of(i)):
                    lanes = lanes_of(scal[at + HEAD0] + s)
                    for x, (source, place) in enumerate(zip(sources, places)):
                        act(pltpu.make_async_copy(
                            source.at[source_rows, lanes], place.at[slot, u, to, :], own_sems.at[slot, u, x]
                        ))

    @pl.when(pairs > 0)
    def _():
        own_copies(0, lambda copy: copy.start())

    def two_heads(n, i, carry):
        slot = lax.rem(i, 2)

        @pl.when(i + 1 < pairs)
        def _():
            own_copies(i + 1, lambda copy: copy.start())

        heads = heads_of(i)

        def foreign(t, group):
            to = rows_of(rows // TILE + scal[at + FAR_TO] + t, group)
            for u, s in enumerate(heads):
                item = pl.ds(scal[at + SOURCE] + offset + s * scal[at + FAR] + t, group)
                for x, place in enumerate(places):
                    part = items[item, x * TILE : (x + 1) * TILE]
                    place[slot, u, to, :] = part.reshape(group * TILE, HD)

        in_groups(0, scal[at + FAR], foreign)
        own_copies(i, lambda copy: copy.wait())
        width = n * BLK
        if width == rows:

            @pl.when((left + right) * TILE > rows)
            def _():
                row = lax.broadcasted_iota(jnp.int32, (TILE, HD), 0)
                for place in places:
                    for u in range(2):
                        first = place[slot, u, rows : rows + TILE, :]
                        last = place[slot, u, 2 * rows : 2 * rows + TILE, :]
                        place[slot, u, rows : rows + TILE, :] = jnp.where(row < lead, last, first)

        place = lax.broadcasted_iota(jnp.int32, (1, width), 1)
        valid = ((place >= lead) & (place < end)) | (place + rows < end)
        bias = jnp.where(valid, 0.0, NEG)
        ones = jnp.ones((width, HD), jnp.bfloat16)
        qs, ks, vs = places
        whole = slice(rows, rows + width)
        for j in range(n):
            mine = slice(rows + j * BLK, rows + (j + 1) * BLK)
            for u, s in enumerate(heads):
                v_ones = jnp.concatenate([vs[slot, u, whole, :], ones], axis=1)
                o_ref[j * BLK : (j + 1) * BLK, lanes_of(scal[at + HEAD0] + s)] = attend_rows(
                    qs[slot, u, mine, :], ks[slot, u, whole, :], v_ones, lambda x: x + bias
                )
        return carry

    for n in range(1, rows // BLK + 1):

        @pl.when((blocks == n) & (pairs > 0))
        def _(n=n):
            o_ref[0 : n * BLK, :] = jnp.zeros((n * BLK, o_ref.shape[1]), o_ref.dtype)
            lax.fori_loop(0, pairs, functools.partial(two_heads, n), 0)
            projected(o_ref, w_ref, zz, n * BLK)
            zz[rows : 2 * rows, :] = zz[0:rows, :]

    @pl.when(pairs <= 0)
    def _():
        zz[...] = jnp.zeros_like(zz)

    return zz[pl.ds(pl.multiple_of(left * TILE, TILE), rows), :]


def fetch(scal, at, offset, low, high, places, boxes, items, sems):
    begin = scal[at + SOURCE] + offset + low * scal[at + FAR]
    end = scal[at + SOURCE] + offset + high * scal[at + FAR]
    return [
        (
            pltpu.make_async_copy(box, items.at[pl.ds(place, box.shape[0])], sems.at[i]),
            (high > low) & (begin < place + box.shape[0]) & (end > place),
        )
        for i, (place, box) in enumerate(zip(places, boxes))
    ]


def clear(places, rows):
    for place in places:
        for slot in range(2):
            for u in range(2):
                place[slot, u, rows : 2 * rows + TILE, :] = jnp.zeros((rows + TILE, HD), place.dtype)


def of_boundary(scal, at, shape, mine):
    row = lax.broadcasted_iota(jnp.int32, shape, 0)
    tail = jnp.where(row >= shape[0] - scal[at + LROWS], 1, 0)
    head = jnp.where(row < scal[at + RROWS], 1, 0)
    right_is_mine = (scal[at + SIDE] == 0) == mine
    return jnp.where(right_is_mine, head, tail) == 1


def send_back(scal, at, z, back_ref):
    lane = lax.broadcasted_iota(jnp.int32, z.shape, 1)
    back = jnp.where(of_boundary(scal, at, z.shape, False), z, 0.0)
    high = back.astype(jnp.bfloat16).astype(jnp.float32)
    both = jnp.where(lane == HD // 2 + 1, pltpu.roll(back - high, 1, 1), high)
    back_ref[...] = both.T[: back_ref.shape[0]].astype(jnp.bfloat16)


def early_kernel(places, at, scal, q_hbm, k_hbm, v_hbm, w_ref, *rest):
    boxes, (out_ref, items, sems, own_sems, qs, ks, vs, o_ref, zz) = rest[: len(places)], rest[len(places) :]
    high = scal[at + EARLY]
    copies = fetch(scal, at, 0, 0, high, places, boxes, items, sems)
    for copy, need in copies:
        pl.when(need)(copy.start)
    clear((qs, ks, vs), zz.shape[0] // 2)
    for copy, need in copies:
        pl.when(need)(copy.wait)
    out_ref[...] = across(
        scal, at, 0, 0, high, (q_hbm, k_hbm, v_hbm), items, w_ref, own_sems, (qs, ks, vs), o_ref, zz
    )


def last_kernel(places, offsets, scal, q_hbm, k_hbm, v_hbm, w_ref, *rest):
    partials, rest = rest[:4], rest[4:]
    boxes, rest = rest[: len(places)], rest[len(places) :]
    own_ref, pass_back_ref, direct_back_ref, items, sems, own_sems, qs, ks, vs, o_ref, zz, sums, sum_sems = rest
    sum_copies = [
        pltpu.make_async_copy(part, sums.at[i], sum_sems.at[i]) for i, part in enumerate(partials)
    ]
    for copy in sum_copies:
        copy.start()
    clear((qs, ks, vs), zz.shape[0] // 2)

    def remaining(at, offset):
        low, high = scal[at + EARLY], scal[at + KEEP]
        copies = fetch(scal, at, offset, low, high, places, boxes, items, sems)
        for copy, need in copies:
            pl.when(need)(copy.start)
        for copy, need in copies:
            pl.when(need)(copy.wait)
        return across(
            scal, at, offset, low, high, (q_hbm, k_hbm, v_hbm), items, w_ref, own_sems, (qs, ks, vs), o_ref, zz
        )

    passed_z = remaining(PASS, offsets[0])
    for copy in sum_copies:
        copy.wait()
    passed_z = passed_z + sums[0]
    send_back(scal, PASS, passed_z, pass_back_ref)
    own = jnp.where(of_boundary(scal, PASS, passed_z.shape, True), passed_z, sums[2] + sums[3])
    direct_z = sums[1] + remaining(DIRECT, offsets[1])
    send_back(scal, DIRECT, direct_z, direct_back_ref)
    own = jnp.where(of_boundary(scal, DIRECT, own.shape, True), direct_z, own)
    own_ref[...] = own.T[: own_ref.shape[0]]


def step_rows(video_ids, step_sizes):
    chosen = video_ids[:, None] == jnp.arange(step_sizes.shape[0], dtype=jnp.int32)[None, :]
    return jnp.sum(jnp.where(chosen, step_sizes[None, :], 0.0), axis=1)


def call(kernel, name, mib, scalars, operands, in_specs, outs, out_specs, scratch, grid=()):
    return pl.pallas_call(
        kernel,
        out_shape=outs,
        grid_spec=pltpu.PrefetchScalarGridSpec(
            num_scalar_prefetch=1, grid=grid, in_specs=in_specs, out_specs=out_specs,
            scratch_shapes=scratch,
        ),
        compiler_params=pltpu.CompilerParams(vmem_limit_bytes=mib * MIB),
        cost_estimate=pl.CostEstimate(flops=1, bytes_accessed=1, transcendentals=0),
        name=name,
    )(scalars, *operands)


def per_device(
    query_rows, key_rows, value_rows, positions, latents, w_head, modulation,
    guide_scale, step_sizes, lengths,
):
    rows, features = query_rows.shape[1], query_rows.shape[2]
    heads = features // HD
    count = lax.axis_size("req")
    here = lax.axis_index("req")
    first_row = here * rows
    _, padded, room = sizes(rows, heads)
    chunk = padded // CHUNKS
    late_sizes = (*[chunk] * (CHUNKS - 1), MORE, room - padded - MORE)

    angle = angles(positions)
    odd = (jnp.arange(HD, dtype=jnp.int32) % 2).astype(jnp.float32)
    cosine = jnp.cos(angle)
    sine = jnp.sin(angle) * (2.0 * odd - 1.0)[None, :]

    smem = pl.BlockSpec(memory_space=pltpu.SMEM)
    vmem = pl.BlockSpec(memory_space=pltpu.VMEM)
    hbm = pl.BlockSpec(memory_space=pl.ANY)
    parity = lax.axis_index("cfg")
    tie = lax.optimization_barrier
    scalars = pl.pallas_call(
        functools.partial(plan_kernel, rows, heads, count),
        out_shape=jax.ShapeDtypeStruct((SCALARS,), jnp.int32),
        in_specs=[smem],
        out_specs=smem,
        scratch_shapes=[
            pltpu.SMEM((count + 8,), jnp.int32),
            pltpu.SMEM((count + 8,), jnp.int32),
            pltpu.VMEM(((count + 8) * 8, 128), jnp.float32),
            pltpu.VMEM(((count + 8) * 8, 128), jnp.float32),
        ],
        name="plan",
    )(lengths)

    def in_hbm(x):
        return pltpu.with_memory_space_constraint(x, pltpu.HBM)

    q, k, v = query_rows[0], key_rows[0], value_rows[0]

    def box(items):
        return jax.ShapeDtypeStruct((items, 3 * TILE, HD), jnp.bfloat16)

    def box_scratch(items):
        return pltpu.VMEM((items, 3 * TILE, HD), jnp.bfloat16)

    group = next(n for n in (5, 4, 3, 2, 1) if heads % n == 0)
    steps = heads // group
    head_block = pl.BlockSpec((rows, group * HD), lambda g, s: (0, g))
    table = pl.BlockSpec((rows, HD), lambda g, s: (0, 0))
    first = call(
        first_kernel, "pack_first", 16, scalars, (in_hbm(q), in_hbm(k), in_hbm(v), cosine, sine),
        [hbm] * 3 + [vmem] * 2, (box(chunk),), (vmem,),
        [*[pltpu.VMEM((4, rows, HD), jnp.bfloat16)] * 3, pltpu.SemaphoreType.DMA((4, 3))],
    )
    pairs = [(i, i ^ 1) for i in range(count)]
    onward = [(i, i + 2) for i in range(0, count - 2, 2)] + [(i + 2, i) for i in range(1, count - 2, 2)]
    got = [lax.ppermute(first[0], "req", pairs)]

    after_first, _ = tie((scalars, first[0]))
    swap = jnp.asarray(numpy.eye(2 * HD)[numpy.arange(2 * HD) ^ 1], jnp.bfloat16)
    q_rot, k_rot, w_both, shift, *second = call(
        functools.partial(second_kernel, chunk), "turn_and_pack_rest", 32, after_first,
        (in_hbm(q), in_hbm(k), in_hbm(v), cosine, sine, swap, w_head.T, modulation),
        [head_block] * 3 + [table] * 2 + [vmem] * 3,
        (pltpu.HBM(q.shape, q.dtype), pltpu.HBM(k.shape, k.dtype),
         jax.ShapeDtypeStruct((HD, features), jnp.bfloat16),
         jax.ShapeDtypeStruct((HD // 2, HD), jnp.float32),
         *[box(n) for n in late_sizes], box(late_sizes[-1])),
        (head_block, head_block, vmem, vmem, *[hbm] * (len(late_sizes) + 1)),
        [box_scratch(sum(late_sizes)), pltpu.SemaphoreType.DMA((len(late_sizes),))], grid=(steps,),
    )
    got += [lax.ppermute(x, "req", pairs) for x in second[: CHUNKS - 1]]
    more, arriving = second[CHUNKS:]

    own_rows = first_row + jnp.arange(rows, dtype=jnp.int32)
    video = jnp.sum((jnp.cumsum(lengths)[None, :] <= own_rows[:, None]).astype(jnp.int32), axis=1)
    step_of_row = step_rows(video, step_sizes)

    def inner(when, first_step, step_count):
        block = pl.BlockSpec((rows, group * HD), lambda g, s: (0, g + first_step))
        width = step_count * group * HD
        return call(
            inner_kernel, "inner_videos", 20, when,
            (in_hbm(q_rot), in_hbm(k_rot), in_hbm(v), w_both, video[:, None], video[None, :]),
            [block] * 3 + [pl.BlockSpec((HD, width), lambda g, s: (0, first_step // step_count))] + [vmem] * 2, pltpu.HBM((rows, HD), jnp.float32), vmem,
            [pltpu.VMEM((rows, width), jnp.bfloat16)], grid=(step_count,),
        )

    got[1], second[CHUNKS - 1] = tie((got[1], second[CHUNKS - 1]))
    got.append(lax.ppermute(second[CHUNKS - 1], "req", pairs))
    when_a, got[0] = tie((scalars, got[0]))
    inner_a = inner(when_a, 0, steps // 2)
    got[1], inner_a = tie((got[1], inner_a))
    passed = [lax.ppermute(x, "req", onward) for x in got[:2]]
    when_b, passed[0], got[2], inner_a = tie((scalars, passed[0], got[2], inner_a))
    inner_b = inner(when_b, steps // 2, steps - steps // 2)
    got[3], inner_b = tie((got[3], inner_b))
    when_early, got[3] = tie((scalars, got[3]))
    passed += [lax.ppermute(x, "req", onward) for x in got[2:CHUNKS]]

    place = pltpu.VMEM((2, 2, 3 * rows, HD), jnp.bfloat16)
    work = [
        pltpu.SemaphoreType.DMA((2, 2, 3)), place, place, place,
        pltpu.VMEM((rows, features), jnp.bfloat16),
        pltpu.VMEM((2 * rows, HD), jnp.float32),
    ]
    partial = pltpu.HBM((rows, HD), jnp.float32)
    lanes = HD // 2 + TILE
    sent_back = jax.ShapeDtypeStruct((lanes, rows), jnp.bfloat16)

    def on_videos_across(kernel, name, when, boxes, outs, others=(), scratch=()):
        places = [0]
        for x in boxes:
            places.append(places[-1] + x.shape[0])
        return call(
            kernel(tuple(places[:-1])), name, 32, when,
            (in_hbm(q_rot), in_hbm(k_rot), in_hbm(v), w_both, *[in_hbm(x) for x in others], *boxes),
            [hbm] * 3 + [vmem] + [hbm] * (len(others) + len(boxes)),
            outs, jax.tree.map(lambda _: vmem, outs),
            [box_scratch(places[-1]), pltpu.SemaphoreType.DMA((len(boxes),)), *work, *scratch],
        )

    def early_on(at, name, when, boxes):
        return on_videos_across(
            lambda places: functools.partial(early_kernel, places, at), name, when, boxes,
            partial,
        )

    early = early_on(PASS, "videos_across_early", when_early, passed[:EARLY_CHUNKS])
    when_direct, early, passed[2] = tie((scalars, early, passed[2]))
    direct_z = early_on(DIRECT, "videos_across_direct", when_direct, got)

    pieces = jnp.maximum(scalars[MOST] - padded - MORE + EXTRA - 1, 0) // EXTRA
    pieces, direct_z = tie((pieces, direct_z))

    def one_more(i, arrived):
        piece = lax.dynamic_slice_in_dim(more, i * EXTRA, EXTRA, 0)
        piece = lax.ppermute(piece, "req", pairs)
        return lax.dynamic_update_slice_in_dim(arrived, piece, i * EXTRA, 0)

    arrived = lax.fori_loop(0, pieces, one_more, arriving)
    before = EARLY_CHUNKS - 1
    offsets = (-chunk * before, chunk * (CHUNKS - before))
    own, to_beyond, to_direct = on_videos_across(
        lambda places: functools.partial(last_kernel, places, offsets), "videos_across_last", scalars,
        [*passed[before:], *got, arrived],
        (jax.ShapeDtypeStruct((lanes, rows), jnp.float32), sent_back, sent_back),
        (early, direct_z, inner_a, inner_b),
        (pltpu.VMEM((4, rows, HD), jnp.float32), pltpu.SemaphoreType.DMA((4,))),
    )
    back_direct = lax.ppermute(to_direct, "req", pairs)
    beyond = [(i, i + 1) for i in range(1, count - 1, 2)] + [(i + 1, i) for i in range(1, count - 1, 2)]
    back_beyond = lax.ppermute(to_beyond, "req", beyond)
    total = own + back_direct.astype(jnp.float32) + back_beyond.astype(jnp.float32)
    values = HD // 2
    squares = total[values : values + 1] + total[values + 1 : values + 2]
    velocity = total[:values] * lax.rsqrt(squares / features + 1e-06) + shift[:, :1]

    width = latents.shape[1]
    mine = lax.dynamic_slice_in_dim(velocity, parity * width, width, 0)
    theirs = lax.dynamic_slice_in_dim(velocity, (1 - parity) * width, width, 0)
    partner = lax.ppermute(theirs, "cfg", [(0, 1), (1, 0)])
    conditional = jnp.where(parity == 0, mine, partner)
    unconditional = jnp.where(parity == 0, partner, mine)
    guided = unconditional + guide_scale[0] * (conditional - unconditional)
    return (latents.T + step_of_row[None, :] * guided).T


def solution(mesh):
    in_specs = (
        P("cfg", "req", None), P("cfg", "req", None), P("cfg", "req", None),
        P(None, "req"), P("req", "cfg"), P(), P(), P(), P(), P(),
    )
    return jax.shard_map(
        per_device, mesh=mesh, in_specs=in_specs, out_specs=P("req", "cfg"), check_vma=False
    )
```

profile of v0, /device:TPU:13, one launch (start us, length us, event | category | flops | bytes accessed | tf_op | source)
XLA Modules:
  0.0 105.9 jit_solution(9608611434094090478)
XLA Ops:
  0.1 0.7 convert_element_type.35
  0.8 2.2 %plan.1.scal = s32[48]{0:T(128)} custom-call(s32[32]{0:T(128)} %lengths.1), custom_call_target="tpu_custom_call" | custom-call | tf_op jit(solution)/shard_map/plan/pallas_call | solution.py:628
  3.0 1.0 sine_multiply_fusion
  4.7 2.6 %pack_first.1 = bf16[44,48,128]{2,1,0:T(8,128)(2,1)S(1)} custom-call(s32[48]{0:T(128)S(1)} %copy-done.2, bf16[512,2560]{1,0:T(8,128)(2,1)} %bitcast.38, bf16[512,2560]{1,0:T(8,128)(2,1)} %bitcast.40, bf16[512,2560]{1,0:T(8,128)(2,1)} %bitcast.31, f32[512,128]{1,0:T(8,128)S(1)} %get-tuple-element.107.cos_ref, f32[512,128]{1,0:T(8,128)S(1)} %get-tuple-element.106.sin_ref), custom_call_target="tpu_custom_call" | custom-call | flops 1 | bytes 1 | tf_op jit(solution)/shard_map/pack_first/pallas_call | solution.py:592
  7.3 2.2 %collective-permute-start.2 = (bf16[44,48,128]{2,1,0:T(8,128)(2,1)S(1)}, bf16[44,48,128]{2,1,0:T(8,128)(2,1)S(1)}, u32[]{:S(2)}, u32[]{:S(2)}) collective-permute-start(bf16[44,48,128]{2,1,0:T(8,128)(2,1)S(1)} %pack_first.1), channel_id=1, source_target_pairs={{0,1},{1,0},{2,3},{3,2},{4,5},{5,4},{6,7},{7,6},{8,9},{9,8},{10,11... | collective-permute-start | bytes 1622024 | tf_op jit(solution)/shard_map/ppermute | solution.py:664
  9.6 11.0 %turn_and_pack_rest.1 = (bf16[512,2560]{1,0:T(8,128)(2,1)}, bf16[512,2560]{1,0:T(8,128)(2,1)}, bf16[128,2560]{1,0:T(8,128)(2,1)S(1)}, f32[64,128]{1,0:T(8,128)S(...) custom-call(s32[48]{0:T(128)S(1)} %copy-done.3, ...), custom_call_target="tpu_custom_call" | custom-call | flops 1 | bytes 1 | tf_op jit(solution)/shard_map/turn_and_pack_rest/pallas_call | solution.py:592
  20.7 1.4 %collective-permute-start.4 = (bf16[44,48,128]{2,1,0:T(8,128)(2,1)}, bf16[44,48,128]{2,1,0:T(8,128)(2,1)S(1)}, u32[]{:S(2)}, u32[]{:S(2)}) collective-permute-start(bf16[44,48,128]{2,1,0:T(8,128)(2,1)} %get-tuple-element.67), channel_id=1, source_target_pairs={{0,1},{1,0},{2,3},{3,2},{4,5},{5,4},{6,7},{7,6},{8,9},{9,8},{10,11... | collective-permute-start | bytes 1622024 | tf_op jit(solution)/shard_map/ppermute | solution.py:679
  22.1 4.6 %collective-permute-start.3 = (bf16[44,48,128]{2,1,0:T(8,128)(2,1)S(1)}, bf16[44,48,128]{2,1,0:T(8,128)(2,1)}, u32[]{:S(2)}, u32[]{:S(2)}) collective-permute-start(bf16[44,48,128]{2,1,0:T(8,128)(2,1)S(1)} %collective-permute-done.2.rest_0_.rest_7_), channel_id=1, source_target_pairs={{0,2},{2,4},{4,6},{6,8},{8,10},{10,12},{12,14},{3,1},{5,3},{7,5},{... | collective-permute-start | bytes 1622024 | tf_op jit(solution)/shard_map/ppermute | solution.py:701
  27.1 6.5 %collective-permute-done.5.rest_1_.rest_8_ = bf16[44,48,128]{2,1,0:T(8,128)(2,1)S(1)} collective-permute-done((bf16[44,48,128]{2,1,0:T(8,128)(2,1)S(1)}, bf16[44,48,128]{2,1,0:T(8,128)(2,1)S(1)}, u32[]{:S(2)}, u32[]{:S(2)}) %collective-permute-start.5) | collective-permute-done | bytes 540704 | tf_op jit(solution)/shard_map/ppermute | solution.py:679
  33.5 1.3 %collective-permute-start.8 = (bf16[48,48,128]{2,1,0:T(8,128)(2,1)}, bf16[48,48,128]{2,1,0:T(8,128)(2,1)S(1)}, u32[]{:S(2)}, u32[]{:S(2)}) collective-permute-start(bf16[48,48,128]{2,1,0:T(8,128)(2,1)} %get-tuple-element.82), channel_id=1, source_target_pairs={{0,1},{1,0},{2,3},{3,2},{4,5},{5,4},{6,7},{7,6},{8,9},{9,8},{10,11... | collective-permute-start | bytes 1769480 | tf_op jit(solution)/shard_map/ppermute | solution.py:697
  35.1 7.7 %inner_videos.2.rest_2_ = f32[512,128]{1,0:T(8,128)} custom-call(s32[48]{0:T(128)S(1)} %copy-done.3, bf16[512,2560]{1,0:T(8,128)(2,1)} %get-tuple-element.62.q_ref.q_hbm, bf16[512,2560]{1,0:T(8,128)(2,1)} %get-tuple-element.63.k_ref.k_hbm, bf16[512,2560]{1,0:T(8,128)(2,1)} %bitcast.33, bf16[128,2560]{1,0:T(8,128)(2,1)S(1)} %get-tuple-element.64.w_ref, ...), custom_call_target="tpu_custom_call" | custom-call | flops 1 | bytes 1 | tf_op jit(solution)/shard_map/inner_videos/pallas_call | solution.py:592
  42.8 4.5 %collective-permute-start.6 = (bf16[44,48,128]{2,1,0:T(8,128)(2,1)S(1)}, bf16[44,48,128]{2,1,0:T(8,128)(2,1)}, u32[]{:S(2)}, u32[]{:S(2)}) collective-permute-start(bf16[44,48,128]{2,1,0:T(8,128)(2,1)S(1)} %collective-permute-done.5.rest_1_.rest_8_), channel_id=1, source_target_pairs={{0,2},{2,4},{4,6},{6,8},{8,10},{10,12},{12,14},{3,1},{5,3},{7,5},{... | collective-permute-start | bytes 1622024 | tf_op jit(solution)/shard_map/ppermute | solution.py:701
  47.3 2.3 %collective-permute-start.7 = (bf16[44,48,128]{2,1,0:T(8,128)(2,1)S(1)}, bf16[44,48,128]{2,1,0:T(8,128)(2,1)}, u32[]{:S(2)}, u32[]{:S(2)}) collective-permute-start(bf16[44,48,128]{2,1,0:T(8,128)(2,1)S(1)} %collective-permute-done.4.rest_2_.rest_9_), channel_id=1, source_target_pairs={{0,2},{2,4},{4,6},{6,8},{8,10},{10,12},{12,14},{3,1},{5,3},{7,5},{... | collective-permute-start | bytes 1622024 | tf_op jit(solution)/shard_map/ppermute | solution.py:706
  51.5 7.7 %inner_videos.3.rest_3_ = f32[512,128]{1,0:T(8,128)} custom-call(s32[48]{0:T(128)S(1)} %copy-done.3, bf16[512,2560]{1,0:T(8,128)(2,1)} %get-tuple-element.62.q_ref.q_hbm, bf16[512,2560]{1,0:T(8,128)(2,1)} %get-tuple-element.63.k_ref.k_hbm, bf16[512,2560]{1,0:T(8,128)(2,1)} %bitcast.34, bf16[128,2560]{1,0:T(8,128)(2,1)S(1)} %get-tuple-element.64.w_ref, ...), custom_call_target="tpu_custom_call" | custom-call | flops 1 | bytes 1 | tf_op jit(solution)/shard_map/inner_videos/pallas_call | solution.py:592
  59.3 3.1 %collective-permute-start.9 = (bf16[44,48,128]{2,1,0:T(8,128)(2,1)}, bf16[44,48,128]{2,1,0:T(8,128)(2,1)}, u32[]{:S(2)}, u32[]{:S(2)}) collective-permute-start(bf16[44,48,128]{2,1,0:T(8,128)(2,1)} %collective-permute-done.1.rest_3_.rest_10_), channel_id=1, source_target_pairs={{0,2},{2,4},{4,6},{6,8},{8,10},{10,12},{12,14},{3,1},{5,3},{7,5},{... | collective-permute-start | bytes 1622024 | tf_op jit(solution)/shard_map/ppermute | solution.py:706
  62.4 14.0 %videos_across_early.1.rest_0_ = f32[512,128]{1,0:T(8,128)} custom-call(s32[48]{0:T(128)S(1)} %copy-done.3, bf16[512,2560]{1,0:T(8,128)(2,1)} %get-tuple-element.62.q_ref.q_hbm, bf16[512,2560]{1,0:T(8,128)(2,1)} %get-tuple-element.63.k_ref.k_hbm, bf16[512,2560]{1,0:T(8,128)(2,1)} %bitcast.35, bf16[128,2560]{1,0:T(8,128)(2,1)S(1)} %get-tuple-element.64.w_ref, ...), custom_call_target="tpu_custom_call" | custom-call | flops 1 | bytes 1 | tf_op jit(solution)/shard_map/videos_across_early/pallas_call | solution.py:592
  76.4 6.9 %videos_across_direct.1.rest_1_ = f32[512,128]{1,0:T(8,128)} custom-call(s32[48]{0:T(128)S(1)} %copy-done.3, bf16[512,2560]{1,0:T(8,128)(2,1)} %get-tuple-element.62.q_ref.q_hbm, bf16[512,2560]{1,0:T(8,128)(2,1)} %get-tuple-element.63.k_ref.k_hbm, bf16[512,2560]{1,0:T(8,128)(2,1)} %bitcast.36, bf16[128,2560]{1,0:T(8,128)(2,1)S(1)} %get-tuple-element.64.w_ref, ...), custom_call_target="tpu_custom_call" | custom-call | flops 1 | bytes 1 | tf_op jit(solution)/shard_map/videos_across_direct/pallas_call | solution.py:592
  83.3 2.7 %videos_across_last.1 = (f32[80,512]{1,0:T(8,128)S(1)}, bf16[80,512]{1,0:T(8,128)(2,1)S(1)}, bf16[80,512]{1,0:T(8,128)(2,1)S(1)}) custom-call(s32[48]{0:T(128)S(1)} %copy-done.3, bf16[512,2560]{1,0:T(8,128)(2,1)} %get-tuple-element.62.q_ref.q_hbm, bf16[512,2560]{1,0:T(8,128)(2,1)} %get-tuple-element.63.k_ref.k_hbm, bf16[512,2560]{1,0:T(8,128)(2,1)} %bitcast.37, ...), custom_call_target="tpu_custom_call" | custom-call | flops 1 | bytes 1 | tf_op jit(solution)/shard_map/videos_across_last/pallas_call | solution.py:592
  86.1 4.9 %collective-permute-start.10 = (bf16[80,512]{1,0:T(8,128)(2,1)S(1)}, bf16[80,512]{1,0:T(8,128)(2,1)S(1)}, u32[]{:S(2)}, u32[]{:S(2)}) collective-permute-start(bf16[80,512]{1,0:T(8,128)(2,1)S(1)} %get-tuple-element.92), channel_id=1, source_target_pairs={{0,1},{1,0},{2,3},{3,2},{4,5},{5,4},{6,7},{7,6},{8,9},{9,8},{10,11... | collective-permute-start | bytes 245768 | tf_op jit(solution)/shard_map/ppermute | solution.py:758
  91.0 1.9 %collective-permute-start.11 = (bf16[80,512]{1,0:T(8,128)(2,1)S(1)}, bf16[80,512]{1,0:T(8,128)(2,1)S(1)}, u32[]{:S(2)}, u32[]{:S(2)}) collective-permute-start(bf16[80,512]{1,0:T(8,128)(2,1)S(1)} %get-tuple-element.93), channel_id=1, source_target_pairs={{1,2},{3,4},{5,6},{7,8},{9,10},{11,12},{13,14},{2,1},{4,3},{6,5},{... | collective-permute-start | bytes 245768 | tf_op jit(solution)/shard_map/ppermute | solution.py:760
  93.0 4.0 %collective-permute-done.11 = bf16[80,512]{1,0:T(8,128)(2,1)S(1)} collective-permute-done((bf16[80,512]{1,0:T(8,128)(2,1)S(1)}, bf16[80,512]{1,0:T(8,128)(2,1)S(1)}, u32[]{:S(2)}, u32[]{:S(2)}) %collective-permute-start.11) | collective-permute-done | bytes 81952 | tf_op jit(solution)/shard_map/ppermute | solution.py:760
  97.2 7.1 %collective-permute-start.12 = (f32[32,512]{1,0:T(8,128)S(1)}, f32[32,512]{1,0:T(8,128)S(1)}, u32[]{:S(2)}, u32[]{:S(2)}) collective-permute-start(f32[32,512]{1,0:T(8,128)S(1)} %constant_dynamic-slice_fusion.1), channel_id=1, source_target_pairs={{0,16},{16,0},{1,17},{17,1},{2,18},{18,2},{3,19},{19,3},{4,20},{20... | collective-permute-start | bytes 196616 | tf_op jit(solution)/shard_map/ppermute | solution.py:769
  104.4 0.8 collective-permute-done.12
  105.3 0.7 fusion.2
  (47 shorter events, 2.4 us)
Async XLA Ops:
  4.0 0.7 copy-start.2
  4.7 4.9 %copy-start = (bf16[2560,64]{0,1:T(8,128)(2,1)S(1)}, bf16[2560,64]{0,1:T(8,128)(2,1)}, u32[]{:S(2)}) copy-start(bf16[2560,64]{0,1:T(8,128)(2,1)} %param.18) | copy-start | bytes 983044
  4.7 4.9 %copy-start.1 = (bf16[256,256]{1,0:T(8,128)(2,1)S(1)}, bf16[256,256]{1,0:T(8,128)(2,1)}, u32[]{:S(2)}) copy-start(bf16[256,256]{1,0:T(8,128)(2,1)} %constant.125.clone.swap_ref) | copy-start | bytes 393220
  4.7 4.9 %copy-start.3 = (s32[48]{0:T(128)S(1)}, s32[48]{0:T(128)}, u32[]{:S(2)}) copy-start(s32[48]{0:T(128)} %plan.1.scal) | copy-start | bytes 580
  4.7 4.9 %copy-start.4 = (f32[2,2560]{1,0:T(2,128)S(1)}, f32[2,2560]{1,0:T(2,128)}, u32[]{:S(2)}) copy-start(f32[2,2560]{1,0:T(2,128)} %mod_ref.1) | copy-start | bytes 61444
  7.3 14.8 %collective-permute-start.2 = (bf16[44,48,128]{2,1,0:T(8,128)(2,1)S(1)}, bf16[44,48,128]{2,1,0:T(8,128)(2,1)S(1)}, u32[]{:S(2)}, u32[]{:S(2)}) collective-permute-start(bf16[44,48,128]{2,1,0:T(8,128)(2,1)S(1)} %pack_first.1), channel_id=1, source_target_pairs={{0,1},{1,0},{2,3},{3,2},{4,5},{5,4},{6,7},{7,6},{8,9},{9,8},{10,11... | collective-permute-start | bytes 1622024 | tf_op jit(solution)/shard_map/ppermute | solution.py:664
  9.6 17.2 %copy-start.6 = (s32[32]{0:T(128)S(1)}, s32[32]{0:T(128)}, u32[]{:S(2)}) copy-start(s32[32]{0:T(128)} %lengths.1) | copy-start | bytes 388
  20.5 13.0 %collective-permute-start.5 = (bf16[44,48,128]{2,1,0:T(8,128)(2,1)S(1)}, bf16[44,48,128]{2,1,0:T(8,128)(2,1)S(1)}, u32[]{:S(2)}, u32[]{:S(2)}) collective-permute-start(bf16[44,48,128]{2,1,0:T(8,128)(2,1)S(1)} %get-tuple-element.68), channel_id=1, source_target_pairs={{0,1},{1,0},{2,3},{3,2},{4,5},{5,4},{6,7},{7,6},{8,9},{9,8},{10,11... | collective-permute-start | bytes 1622024 | tf_op jit(solution)/shard_map/ppermute | solution.py:679
  20.7 26.6 %collective-permute-start.4 = (bf16[44,48,128]{2,1,0:T(8,128)(2,1)}, bf16[44,48,128]{2,1,0:T(8,128)(2,1)S(1)}, u32[]{:S(2)}, u32[]{:S(2)}) collective-permute-start(bf16[44,48,128]{2,1,0:T(8,128)(2,1)} %get-tuple-element.67), channel_id=1, source_target_pairs={{0,1},{1,0},{2,3},{3,2},{4,5},{5,4},{6,7},{7,6},{8,9},{9,8},{10,11... | collective-permute-start | bytes 1622024 | tf_op jit(solution)/shard_map/ppermute | solution.py:679
  22.1 25.2 %collective-permute-start.3 = (bf16[44,48,128]{2,1,0:T(8,128)(2,1)S(1)}, bf16[44,48,128]{2,1,0:T(8,128)(2,1)}, u32[]{:S(2)}, u32[]{:S(2)}) collective-permute-start(bf16[44,48,128]{2,1,0:T(8,128)(2,1)S(1)} %collective-permute-done.2.rest_0_.rest_7_), channel_id=1, source_target_pairs={{0,2},{2,4},{4,6},{6,8},{8,10},{10,12},{12,14},{3,1},{5,3},{7,5},{... | collective-permute-start | bytes 1622024 | tf_op jit(solution)/shard_map/ppermute | solution.py:701
  26.7 32.6 %collective-permute-start.1 = (bf16[44,48,128]{2,1,0:T(8,128)(2,1)}, bf16[44,48,128]{2,1,0:T(8,128)(2,1)}, u32[]{:S(2)}, u32[]{:S(2)}) collective-permute-start(bf16[44,48,128]{2,1,0:T(8,128)(2,1)} %get-tuple-element.65), channel_id=1, source_target_pairs={{0,1},{1,0},{2,3},{3,2},{4,5},{5,4},{6,7},{7,6},{8,9},{9,8},{10,11... | collective-permute-start | bytes 1622024 | tf_op jit(solution)/shard_map/ppermute | solution.py:679
  33.5 42.9 %collective-permute-start.8 = (bf16[48,48,128]{2,1,0:T(8,128)(2,1)}, bf16[48,48,128]{2,1,0:T(8,128)(2,1)S(1)}, u32[]{:S(2)}, u32[]{:S(2)}) collective-permute-start(bf16[48,48,128]{2,1,0:T(8,128)(2,1)} %get-tuple-element.82), channel_id=1, source_target_pairs={{0,1},{1,0},{2,3},{3,2},{4,5},{5,4},{6,7},{7,6},{8,9},{9,8},{10,11... | collective-permute-start | bytes 1769480 | tf_op jit(solution)/shard_map/ppermute | solution.py:697
  42.8 19.6 %collective-permute-start.6 = (bf16[44,48,128]{2,1,0:T(8,128)(2,1)S(1)}, bf16[44,48,128]{2,1,0:T(8,128)(2,1)}, u32[]{:S(2)}, u32[]{:S(2)}) collective-permute-start(bf16[44,48,128]{2,1,0:T(8,128)(2,1)S(1)} %collective-permute-done.5.rest_1_.rest_8_), channel_id=1, source_target_pairs={{0,2},{2,4},{4,6},{6,8},{8,10},{10,12},{12,14},{3,1},{5,3},{7,5},{... | collective-permute-start | bytes 1622024 | tf_op jit(solution)/shard_map/ppermute | solution.py:701
  47.3 29.1 %collective-permute-start.7 = (bf16[44,48,128]{2,1,0:T(8,128)(2,1)S(1)}, bf16[44,48,128]{2,1,0:T(8,128)(2,1)}, u32[]{:S(2)}, u32[]{:S(2)}) collective-permute-start(bf16[44,48,128]{2,1,0:T(8,128)(2,1)S(1)} %collective-permute-done.4.rest_2_.rest_9_), channel_id=1, source_target_pairs={{0,2},{2,4},{4,6},{6,8},{8,10},{10,12},{12,14},{3,1},{5,3},{7,5},{... | collective-permute-start | bytes 1622024 | tf_op jit(solution)/shard_map/ppermute | solution.py:706
  59.3 24.1 %collective-permute-start.9 = (bf16[44,48,128]{2,1,0:T(8,128)(2,1)}, bf16[44,48,128]{2,1,0:T(8,128)(2,1)}, u32[]{:S(2)}, u32[]{:S(2)}) collective-permute-start(bf16[44,48,128]{2,1,0:T(8,128)(2,1)} %collective-permute-done.1.rest_3_.rest_10_), channel_id=1, source_target_pairs={{0,2},{2,4},{4,6},{6,8},{8,10},{10,12},{12,14},{3,1},{5,3},{7,5},{... | collective-permute-start | bytes 1622024 | tf_op jit(solution)/shard_map/ppermute | solution.py:706
  83.3 21.0 %copy-start.7 = (f32[32]{0:T(128)S(1)}, f32[32]{0:T(128)}, u32[]{:S(2)}) copy-start(f32[32]{0:T(128)} %param.21) | copy-start | bytes 388
  83.3 21.9 %copy-start.5 = (f32[512,32]{0,1:T(8,128)S(1)}, f32[512,32]{0,1:T(8,128)}, u32[]{:S(2)}) copy-start(f32[512,32]{0,1:T(8,128)} %param.17) | copy-start | bytes 196612
  86.1 7.0 %collective-permute-start.10 = (bf16[80,512]{1,0:T(8,128)(2,1)S(1)}, bf16[80,512]{1,0:T(8,128)(2,1)S(1)}, u32[]{:S(2)}, u32[]{:S(2)}) collective-permute-start(bf16[80,512]{1,0:T(8,128)(2,1)S(1)} %get-tuple-element.92), channel_id=1, source_target_pairs={{0,1},{1,0},{2,3},{3,2},{4,5},{5,4},{6,7},{7,6},{8,9},{9,8},{10,11... | collective-permute-start | bytes 245768 | tf_op jit(solution)/shard_map/ppermute | solution.py:758
  91.0 6.1 %collective-permute-start.11 = (bf16[80,512]{1,0:T(8,128)(2,1)S(1)}, bf16[80,512]{1,0:T(8,128)(2,1)S(1)}, u32[]{:S(2)}, u32[]{:S(2)}) collective-permute-start(bf16[80,512]{1,0:T(8,128)(2,1)S(1)} %get-tuple-element.93), channel_id=1, source_target_pairs={{1,2},{3,4},{5,6},{7,8},{9,10},{11,12},{13,14},{2,1},{4,3},{6,5},{... | collective-permute-start | bytes 245768 | tf_op jit(solution)/shard_map/ppermute | solution.py:760
  97.2 8.0 %collective-permute-start.12 = (f32[32,512]{1,0:T(8,128)S(1)}, f32[32,512]{1,0:T(8,128)S(1)}, u32[]{:S(2)}, u32[]{:S(2)}) collective-permute-start(f32[32,512]{1,0:T(8,128)S(1)} %constant_dynamic-slice_fusion.1), channel_id=1, source_target_pairs={{0,16},{16,0},{1,17},{17,1},{2,18},{18,2},{3,19},{19,3},{4,20},{20... | collective-permute-start | bytes 196616 | tf_op jit(solution)/shard_map/ppermute | solution.py:769
where the time goes:
time: 108 us; the launch traced here: 106 us
  Pallas kernels  54.8 us (51%)
  starting transfers between devices  33.6 us (31%)
  waiting for transfers between devices  11.3 us (10%)
  other arithmetic  2.91 us (3%)
  local copies, waits for them, and re-layouts  1.64 us (2%)
  between operations  1.59 us (1%)
    pallas_call x7, Pallas kernels, call(): pl.pallas_call(kernel, out_shape=outs, grid_spec=pltpu.PrefetchScalarGrid...  52.6 us
    ppermute x2, starting transfers between devices, per_device(): passed = [lax.ppermute(x, 'req', onward) for x in got[:2]]  9.08 us
    ppermute x1, starting transfers between devices, per_device(): partner = lax.ppermute(theirs, 'cfg', [(0, 1), (1, 0)])  7.15 us
    ppermute x3, waiting for transfers between devices, per_device(): got += [lax.ppermute(x, 'req', pairs) for x in second[:CHUNKS - 1]]  6.48 us
    ppermute x2, starting transfers between devices, per_device(): passed += [lax.ppermute(x, 'req', onward) for x in got[2:CHUNKS]]  5.44 us
    ppermute x1, starting transfers between devices, per_device(): back_direct = lax.ppermute(to_direct, 'req', pairs)  4.93 us
    ppermute x1, waiting for transfers between devices, per_device(): back_beyond = lax.ppermute(to_beyond, 'req', beyond)  4.04 us
    ppermute x1, starting transfers between devices, per_device(): got = [lax.ppermute(first[0], 'req', pairs)]  2.24 us
  transfers between devices with their start and end apart: 12, of which 3 were waited for; matrix products, arithmetic and copies ran while one was open for 1% of the time, Pallas kernels for 45%

commit v1 on v0

--- a/solution.py
+++ b/solution.py
@@ -38,6 +38,12 @@
     )
     padded = -(-cap // TILE) * TILE
     return cap, padded, 2 * padded
+
+
+def pieces_of(padded):
+    first = padded * 3 // 10
+    rest = (padded - first) // (CHUNKS - 1)
+    return (first, padded - first - rest * (CHUNKS - 2), *[rest] * (CHUNKS - 2))
 
 
 def angles(positions):
@@ -165,7 +171,7 @@
         out[at + HEAD0] = 0 if side == 0 else n
         out[at + KEEP] = keep
         source = jnp.where(direct, partner_passes, 0)
-        there = jnp.where(direct, padded + MORE, padded // CHUNKS * EARLY_CHUNKS) - source
+        there = jnp.where(direct, padded + MORE, sum(pieces_of(padded)[:EARLY_CHUNKS])) - source
         out[at + EARLY] = jnp.minimum(keep, lax.div(jnp.maximum(there, 0), jnp.maximum(far, 1)))
         out[at + SOURCE] = source
         out[at + OWN_FROM] = 0 if side == 0 else rows // TILE - lt
@@ -612,8 +618,8 @@
     here = lax.axis_index("req")
     first_row = here * rows
     _, padded, room = sizes(rows, heads)
-    chunk = padded // CHUNKS
-    late_sizes = (*[chunk] * (CHUNKS - 1), MORE, room - padded - MORE)
+    sizes_passed = pieces_of(padded)
+    late_sizes = (*sizes_passed[1:], MORE, room - padded - MORE)
 
     angle = angles(positions)
     odd = (jnp.arange(HD, dtype=jnp.int32) % 2).astype(jnp.float32)
@@ -656,7 +662,7 @@
     table = pl.BlockSpec((rows, HD), lambda g, s: (0, 0))
     first = call(
         first_kernel, "pack_first", 16, scalars, (in_hbm(q), in_hbm(k), in_hbm(v), cosine, sine),
-        [hbm] * 3 + [vmem] * 2, (box(chunk),), (vmem,),
+        [hbm] * 3 + [vmem] * 2, (box(sizes_passed[0]),), (vmem,),
         [*[pltpu.VMEM((4, rows, HD), jnp.bfloat16)] * 3, pltpu.SemaphoreType.DMA((4, 3))],
     )
     pairs = [(i, i ^ 1) for i in range(count)]
@@ -666,7 +672,7 @@
     after_first, _ = tie((scalars, first[0]))
     swap = jnp.asarray(numpy.eye(2 * HD)[numpy.arange(2 * HD) ^ 1], jnp.bfloat16)
     q_rot, k_rot, w_both, shift, *second = call(
-        functools.partial(second_kernel, chunk), "turn_and_pack_rest", 32, after_first,
+        functools.partial(second_kernel, sizes_passed[0]), "turn_and_pack_rest", 32, after_first,
         (in_hbm(q), in_hbm(k), in_hbm(v), cosine, sine, swap, w_head.T, modulation),
         [head_block] * 3 + [table] * 2 + [vmem] * 3,
         (pltpu.HBM(q.shape, q.dtype), pltpu.HBM(k.shape, k.dtype),
@@ -747,7 +753,7 @@
 
     arrived = lax.fori_loop(0, pieces, one_more, arriving)
     before = EARLY_CHUNKS - 1
-    offsets = (-chunk * before, chunk * (CHUNKS - before))
+    offsets = (-sum(sizes_passed[:before]), sum(sizes_passed[before:]))
     own, to_beyond, to_direct = on_videos_across(
         lambda places: functools.partial(last_kernel, places, offsets), "videos_across_last", scalars,
         [*passed[before:], *got, arrived],

time: 108 us -> 116 us (1.074)
  the two profiles are of different devices: /device:TPU:13 before, /device:TPU:17 now
where the time goes in v1:
time: 116 us; the launch traced here: 118 us
  Pallas kernels  50.4 us (43%)
  starting transfers between devices  42.3 us (36%)
  waiting for transfers between devices  19 us (16%)
  other arithmetic  2.9 us (2%)
  local copies, waits for them, and re-layouts  1.71 us (1%)
  between operations  1.62 us (1%)
    pallas_call x7, Pallas kernels, call(): pl.pallas_call(kernel, out_shape=outs, grid_spec=pltpu.PrefetchScalarGrid...  48.3 us
    ppermute x1, starting transfers between devices, per_device(): back_direct = lax.ppermute(to_direct, 'req', pairs)  14.5 us
    ppermute x3, waiting for transfers between devices, per_device(): got += [lax.ppermute(x, 'req', pairs) for x in second[:CHUNKS - 1]]  10.7 us
    ppermute x2, starting transfers between devices, per_device(): passed = [lax.ppermute(x, 'req', onward) for x in got[:2]]  8.07 us
    ppermute x2, starting transfers between devices, per_device(): passed += [lax.ppermute(x, 'req', onward) for x in got[2:CHUNKS]]  6.08 us
    ppermute x3, starting transfers between devices, per_device(): got += [lax.ppermute(x, 'req', pairs) for x in second[:CHUNKS - 1]]  6.07 us
    ppermute x1, waiting for transfers between devices, per_device(): back_beyond = lax.ppermute(to_beyond, 'req', beyond)  4.71 us
    ppermute x1, starting transfers between devices, per_device(): partner = lax.ppermute(theirs, 'cfg', [(0, 1), (1, 0)])  3.31 us
  transfers between devices with their start and end apart: 12, of which 6 were waited for; matrix products, arithmetic and copies ran while one was open for 1% of the time, Pallas kernels for 36%

profile of v1, /device:TPU:17, one launch (start us, length us, event | category | flops | bytes accessed | tf_op | source)
XLA Modules:
  0.0 118.0 jit_solution(16904430164491848628)
XLA Ops:
  0.8 2.2 %plan.1.scal = s32[48]{0:T(128)} custom-call(s32[32]{0:T(128)} %lengths.1), custom_call_target="tpu_custom_call" | custom-call | tf_op jit(solution)/shard_map/plan/pallas_call | solution.py:634
  3.0 1.0 sine_multiply_fusion
  4.7 2.8 %pack_first.1 = bf16[52,48,128]{2,1,0:T(8,128)(2,1)S(1)} custom-call(s32[48]{0:T(128)S(1)} %copy-done.2, bf16[512,2560]{1,0:T(8,128)(2,1)} %bitcast.38, bf16[512,2560]{1,0:T(8,128)(2,1)} %bitcast.40, bf16[512,2560]{1,0:T(8,128)(2,1)} %bitcast.31, f32[512,128]{1,0:T(8,128)S(1)} %get-tuple-element.107.cos_ref, f32[512,128]{1,0:T(8,128)S(1)} %get-tuple-element.106.sin_ref), custom_call_target="tpu_custom_call" | custom-call | flops 1 | bytes 1 | tf_op jit(solution)/shard_map/pack_first/pallas_call | solution.py:598
  7.5 1.2 %collective-permute-start.2 = (bf16[52,48,128]{2,1,0:T(8,128)(2,1)S(1)}, bf16[52,48,128]{2,1,0:T(8,128)(2,1)S(1)}, u32[]{:S(2)}, u32[]{:S(2)}) collective-permute-start(bf16[52,48,128]{2,1,0:T(8,128)(2,1)S(1)} %pack_first.1), channel_id=1, source_target_pairs={{0,1},{1,0},{2,3},{3,2},{4,5},{5,4},{6,7},{7,6},{8,9},{9,8},{10,11... | collective-permute-start | bytes 1916936 | tf_op jit(solution)/shard_map/ppermute | solution.py:670
  8.8 11.0 %turn_and_pack_rest.1 = (bf16[512,2560]{1,0:T(8,128)(2,1)}, bf16[512,2560]{1,0:T(8,128)(2,1)}, bf16[128,2560]{1,0:T(8,128)(2,1)S(1)}, f32[64,128]{1,0:T(8,128)S(...) custom-call(s32[48]{0:T(128)S(1)} %copy-done.3, ...), custom_call_target="tpu_custom_call" | custom-call | flops 1 | bytes 1 | tf_op jit(solution)/shard_map/turn_and_pack_rest/pallas_call | solution.py:598
  20.4 2.5 %collective-permute-done.2.rest_0_.rest_7_ = bf16[52,48,128]{2,1,0:T(8,128)(2,1)S(1)} collective-permute-done((bf16[52,48,128]{2,1,0:T(8,128)(2,1)S(1)}, bf16[52,48,128]{2,1,0:T(8,128)(2,1)S(1)}, u32[]{:S(2)}, u32[]{:S(2)}) %collective-permute-start.2) | collective-permute-done | bytes 639008 | tf_op jit(solution)/shard_map/ppermute | solution.py:670
  22.8 4.0 %collective-permute-start.3 = (bf16[52,48,128]{2,1,0:T(8,128)(2,1)S(1)}, bf16[52,48,128]{2,1,0:T(8,128)(2,1)}, u32[]{:S(2)}, u32[]{:S(2)}) collective-permute-start(bf16[52,48,128]{2,1,0:T(8,128)(2,1)S(1)} %collective-permute-done.2.rest_0_.rest_7_), channel_id=1, source_target_pairs={{0,2},{2,4},{4,6},{6,8},{8,10},{10,12},{12,14},{3,1},{5,3},{7,5},{... | collective-permute-start | bytes 1916936 | tf_op jit(solution)/shard_map/ppermute | solution.py:707
  26.9 3.1 %collective-permute-start.4 = (bf16[41,48,128]{2,1,0:T(8,128)(2,1)}, bf16[41,48,128]{2,1,0:T(8,128)(2,1)}, u32[]{:S(2)}, u32[]{:S(2)}) collective-permute-start(bf16[41,48,128]{2,1,0:T(8,128)(2,1)} %get-tuple-element.67), channel_id=1, source_target_pairs={{0,1},{1,0},{2,3},{3,2},{4,5},{5,4},{6,7},{7,6},{8,9},{9,8},{10,11... | collective-permute-start | bytes 1511432 | tf_op jit(solution)/shard_map/ppermute | solution.py:685
  30.3 3.7 %collective-permute-done.5.rest_1_.rest_8_ = bf16[42,48,128]{2,1,0:T(8,128)(2,1)S(1)} collective-permute-done((bf16[42,48,128]{2,1,0:T(8,128)(2,1)S(1)}, bf16[42,48,128]{2,1,0:T(8,128)(2,1)S(1)}, u32[]{:S(2)}, u32[]{:S(2)}) %collective-permute-start.5) | collective-permute-done | bytes 516128 | tf_op jit(solution)/shard_map/ppermute | solution.py:685
  34.0 1.1 collective-permute-start.8
  35.4 7.7 %inner_videos.2.rest_2_ = f32[512,128]{1,0:T(8,128)} custom-call(s32[48]{0:T(128)S(1)} %copy-done.3, bf16[512,2560]{1,0:T(8,128)(2,1)} %get-tuple-element.62.q_ref.q_hbm, bf16[512,2560]{1,0:T(8,128)(2,1)} %get-tuple-element.63.k_ref.k_hbm, bf16[512,2560]{1,0:T(8,128)(2,1)} %bitcast.33, bf16[128,2560]{1,0:T(8,128)(2,1)S(1)} %get-tuple-element.64.w_ref, ...), custom_call_target="tpu_custom_call" | custom-call | flops 1 | bytes 1 | tf_op jit(solution)/shard_map/inner_videos/pallas_call | solution.py:598
  43.1 4.0 %collective-permute-start.6 = (bf16[42,48,128]{2,1,0:T(8,128)(2,1)S(1)}, bf16[42,48,128]{2,1,0:T(8,128)(2,1)S(1)}, u32[]{:S(2)}, u32[]{:S(2)}) collective-permute-start(bf16[42,48,128]{2,1,0:T(8,128)(2,1)S(1)} %collective-permute-done.5.rest_1_.rest_8_), channel_id=1, source_target_pairs={{0,2},{2,4},{4,6},{6,8},{8,10},{10,12},{12,14},{3,1},{5,3},{7,5},{... | collective-permute-start | bytes 1548296 | tf_op jit(solution)/shard_map/ppermute | solution.py:707
  47.2 2.3 %collective-permute-start.1 = (bf16[41,48,128]{2,1,0:T(8,128)(2,1)}, bf16[41,48,128]{2,1,0:T(8,128)(2,1)}, u32[]{:S(2)}, u32[]{:S(2)}) collective-permute-start(bf16[41,48,128]{2,1,0:T(8,128)(2,1)} %get-tuple-element.65), channel_id=1, source_target_pairs={{0,1},{1,0},{2,3},{3,2},{4,5},{5,4},{6,7},{7,6},{8,9},{9,8},{10,11... | collective-permute-start | bytes 1511432 | tf_op jit(solution)/shard_map/ppermute | solution.py:685
  49.5 1.9 %collective-permute-start.7 = (bf16[41,48,128]{2,1,0:T(8,128)(2,1)}, bf16[41,48,128]{2,1,0:T(8,128)(2,1)}, u32[]{:S(2)}, u32[]{:S(2)}) collective-permute-start(bf16[41,48,128]{2,1,0:T(8,128)(2,1)} %collective-permute-done.4.rest_2_.rest_9_), channel_id=1, source_target_pairs={{0,2},{2,4},{4,6},{6,8},{8,10},{10,12},{12,14},{3,1},{5,3},{7,5},{... | collective-permute-start | bytes 1511432 | tf_op jit(solution)/shard_map/ppermute | solution.py:712
  53.5 7.8 %inner_videos.3.rest_3_ = f32[512,128]{1,0:T(8,128)} custom-call(s32[48]{0:T(128)S(1)} %copy-done.3, bf16[512,2560]{1,0:T(8,128)(2,1)} %get-tuple-element.62.q_ref.q_hbm, bf16[512,2560]{1,0:T(8,128)(2,1)} %get-tuple-element.63.k_ref.k_hbm, bf16[512,2560]{1,0:T(8,128)(2,1)} %bitcast.34, bf16[128,2560]{1,0:T(8,128)(2,1)S(1)} %get-tuple-element.64.w_ref, ...), custom_call_target="tpu_custom_call" | custom-call | flops 1 | bytes 1 | tf_op jit(solution)/shard_map/inner_videos/pallas_call | solution.py:598
  61.2 7.0 %collective-permute-done.1.rest_3_.rest_10_ = bf16[41,48,128]{2,1,0:T(8,128)(2,1)} collective-permute-done((bf16[41,48,128]{2,1,0:T(8,128)(2,1)}, bf16[41,48,128]{2,1,0:T(8,128)(2,1)}, u32[]{:S(2)}, u32[]{:S(2)}) %collective-permute-start.1) | collective-permute-done | bytes 503840 | tf_op jit(solution)/shard_map/ppermute | solution.py:685
  68.2 4.2 %collective-permute-start.9 = (bf16[41,48,128]{2,1,0:T(8,128)(2,1)}, bf16[41,48,128]{2,1,0:T(8,128)(2,1)}, u32[]{:S(2)}, u32[]{:S(2)}) collective-permute-start(bf16[41,48,128]{2,1,0:T(8,128)(2,1)} %collective-permute-done.1.rest_3_.rest_10_), channel_id=1, source_target_pairs={{0,2},{2,4},{4,6},{6,8},{8,10},{10,12},{12,14},{3,1},{5,3},{7,5},{... | collective-permute-start | bytes 1511432 | tf_op jit(solution)/shard_map/ppermute | solution.py:712
  72.4 10.0 %videos_across_early.1.rest_0_ = f32[512,128]{1,0:T(8,128)} custom-call(s32[48]{0:T(128)S(1)} %copy-done.3, bf16[512,2560]{1,0:T(8,128)(2,1)} %get-tuple-element.62.q_ref.q_hbm, bf16[512,2560]{1,0:T(8,128)(2,1)} %get-tuple-element.63.k_ref.k_hbm, bf16[512,2560]{1,0:T(8,128)(2,1)} %bitcast.35, bf16[128,2560]{1,0:T(8,128)(2,1)S(1)} %get-tuple-element.64.w_ref, ...), custom_call_target="tpu_custom_call" | custom-call | flops 1 | bytes 1 | tf_op jit(solution)/shard_map/videos_across_early/pallas_call | solution.py:598
  82.5 6.2 %videos_across_direct.1.rest_1_ = f32[512,128]{1,0:T(8,128)} custom-call(s32[48]{0:T(128)S(1)} %copy-done.3, bf16[512,2560]{1,0:T(8,128)(2,1)} %get-tuple-element.62.q_ref.q_hbm, bf16[512,2560]{1,0:T(8,128)(2,1)} %get-tuple-element.63.k_ref.k_hbm, bf16[512,2560]{1,0:T(8,128)(2,1)} %bitcast.36, bf16[128,2560]{1,0:T(8,128)(2,1)S(1)} %get-tuple-element.64.w_ref, ...), custom_call_target="tpu_custom_call" | custom-call | flops 1 | bytes 1 | tf_op jit(solution)/shard_map/videos_across_direct/pallas_call | solution.py:598
  88.8 2.7 %videos_across_last.1 = (f32[80,512]{1,0:T(8,128)S(1)}, bf16[80,512]{1,0:T(8,128)(2,1)S(1)}, bf16[80,512]{1,0:T(8,128)(2,1)S(1)}) custom-call(s32[48]{0:T(128)S(1)} %copy-done.3, bf16[512,2560]{1,0:T(8,128)(2,1)} %get-tuple-element.62.q_ref.q_hbm, bf16[512,2560]{1,0:T(8,128)(2,1)} %get-tuple-element.63.k_ref.k_hbm, bf16[512,2560]{1,0:T(8,128)(2,1)} %bitcast.37, ...), custom_call_target="tpu_custom_call" | custom-call | flops 1 | bytes 1 | tf_op jit(solution)/shard_map/videos_across_last/pallas_call | solution.py:598
  91.5 14.5 %collective-permute-start.10 = (bf16[80,512]{1,0:T(8,128)(2,1)S(1)}, bf16[80,512]{1,0:T(8,128)(2,1)S(1)}, u32[]{:S(2)}, u32[]{:S(2)}) collective-permute-start(bf16[80,512]{1,0:T(8,128)(2,1)S(1)} %get-tuple-element.92), channel_id=1, source_target_pairs={{0,1},{1,0},{2,3},{3,2},{4,5},{5,4},{6,7},{7,6},{8,9},{9,8},{10,11... | collective-permute-start | bytes 245768 | tf_op jit(solution)/shard_map/ppermute | solution.py:764
  106.0 1.9 %collective-permute-start.11 = (bf16[80,512]{1,0:T(8,128)(2,1)S(1)}, bf16[80,512]{1,0:T(8,128)(2,1)S(1)}, u32[]{:S(2)}, u32[]{:S(2)}) collective-permute-start(bf16[80,512]{1,0:T(8,128)(2,1)S(1)} %get-tuple-element.93), channel_id=1, source_target_pairs={{1,2},{3,4},{5,6},{7,8},{9,10},{11,12},{13,14},{2,1},{4,3},{6,5},{... | collective-permute-start | bytes 245768 | tf_op jit(solution)/shard_map/ppermute | solution.py:766
  108.3 4.7 %collective-permute-done.11 = bf16[80,512]{1,0:T(8,128)(2,1)S(1)} collective-permute-done((bf16[80,512]{1,0:T(8,128)(2,1)S(1)}, bf16[80,512]{1,0:T(8,128)(2,1)S(1)}, u32[]{:S(2)}, u32[]{:S(2)}) %collective-permute-start.11) | collective-permute-done | bytes 81952 | tf_op jit(solution)/shard_map/ppermute | solution.py:766
  113.1 3.3 %collective-permute-start.12 = (f32[32,512]{1,0:T(8,128)S(1)}, f32[32,512]{1,0:T(8,128)S(1)}, u32[]{:S(2)}, u32[]{:S(2)}) collective-permute-start(f32[32,512]{1,0:T(8,128)S(1)} %constant_dynamic-slice_fusion.1), channel_id=1, source_target_pairs={{0,16},{16,0},{1,17},{17,1},{2,18},{18,2},{3,19},{19,3},{4,20},{20... | collective-permute-start | bytes 196616 | tf_op jit(solution)/shard_map/ppermute | solution.py:775
  (47 shorter events, 5.3 us)
Async XLA Ops:
  4.0 0.7 copy-start.2
  4.7 4.1 %copy-start = (bf16[2560,64]{0,1:T(8,128)(2,1)S(1)}, bf16[2560,64]{0,1:T(8,128)(2,1)}, u32[]{:S(2)}) copy-start(bf16[2560,64]{0,1:T(8,128)(2,1)} %param.18) | copy-start | bytes 983044
  4.7 4.1 %copy-start.1 = (bf16[256,256]{1,0:T(8,128)(2,1)S(1)}, bf16[256,256]{1,0:T(8,128)(2,1)}, u32[]{:S(2)}) copy-start(bf16[256,256]{1,0:T(8,128)(2,1)} %constant.125.clone.swap_ref) | copy-start | bytes 393220
  4.7 4.1 %copy-start.3 = (s32[48]{0:T(128)S(1)}, s32[48]{0:T(128)}, u32[]{:S(2)}) copy-start(s32[48]{0:T(128)} %plan.1.scal) | copy-start | bytes 580
  4.7 4.1 %copy-start.4 = (f32[2,2560]{1,0:T(2,128)S(1)}, f32[2,2560]{1,0:T(2,128)}, u32[]{:S(2)}) copy-start(f32[2,2560]{1,0:T(2,128)} %mod_ref.1) | copy-start | bytes 61444
  7.5 15.3 %collective-permute-start.2 = (bf16[52,48,128]{2,1,0:T(8,128)(2,1)S(1)}, bf16[52,48,128]{2,1,0:T(8,128)(2,1)S(1)}, u32[]{:S(2)}, u32[]{:S(2)}) collective-permute-start(bf16[52,48,128]{2,1,0:T(8,128)(2,1)S(1)} %pack_first.1), channel_id=1, source_target_pairs={{0,1},{1,0},{2,3},{3,2},{4,5},{5,4},{6,7},{7,6},{8,9},{9,8},{10,11... | collective-permute-start | bytes 1916936 | tf_op jit(solution)/shard_map/ppermute | solution.py:670
  8.8 21.3 %copy-start.6 = (s32[32]{0:T(128)S(1)}, s32[32]{0:T(128)}, u32[]{:S(2)}) copy-start(s32[32]{0:T(128)} %lengths.1) | copy-start | bytes 388
  19.8 14.2 %collective-permute-start.5 = (bf16[42,48,128]{2,1,0:T(8,128)(2,1)S(1)}, bf16[42,48,128]{2,1,0:T(8,128)(2,1)S(1)}, u32[]{:S(2)}, u32[]{:S(2)}) collective-permute-start(bf16[42,48,128]{2,1,0:T(8,128)(2,1)S(1)} %get-tuple-element.68), channel_id=1, source_target_pairs={{0,1},{1,0},{2,3},{3,2},{4,5},{5,4},{6,7},{7,6},{8,9},{9,8},{10,11... | collective-permute-start | bytes 1548296 | tf_op jit(solution)/shard_map/ppermute | solution.py:685
  22.8 26.7 %collective-permute-start.3 = (bf16[52,48,128]{2,1,0:T(8,128)(2,1)S(1)}, bf16[52,48,128]{2,1,0:T(8,128)(2,1)}, u32[]{:S(2)}, u32[]{:S(2)}) collective-permute-start(bf16[52,48,128]{2,1,0:T(8,128)(2,1)S(1)} %collective-permute-done.2.rest_0_.rest_7_), channel_id=1, source_target_pairs={{0,2},{2,4},{4,6},{6,8},{8,10},{10,12},{12,14},{3,1},{5,3},{7,5},{... | collective-permute-start | bytes 1916936 | tf_op jit(solution)/shard_map/ppermute | solution.py:707
  26.9 22.6 %collective-permute-start.4 = (bf16[41,48,128]{2,1,0:T(8,128)(2,1)}, bf16[41,48,128]{2,1,0:T(8,128)(2,1)}, u32[]{:S(2)}, u32[]{:S(2)}) collective-permute-start(bf16[41,48,128]{2,1,0:T(8,128)(2,1)} %get-tuple-element.67), channel_id=1, source_target_pairs={{0,1},{1,0},{2,3},{3,2},{4,5},{5,4},{6,7},{7,6},{8,9},{9,8},{10,11... | collective-permute-start | bytes 1511432 | tf_op jit(solution)/shard_map/ppermute | solution.py:685
  34.0 48.5 %collective-permute-start.8 = (bf16[48,48,128]{2,1,0:T(8,128)(2,1)}, bf16[48,48,128]{2,1,0:T(8,128)(2,1)S(1)}, u32[]{:S(2)}, u32[]{:S(2)}) collective-permute-start(bf16[48,48,128]{2,1,0:T(8,128)(2,1)} %get-tuple-element.82), channel_id=1, source_target_pairs={{0,1},{1,0},{2,3},{3,2},{4,5},{5,4},{6,7},{7,6},{8,9},{9,8},{10,11... | collective-permute-start | bytes 1769480 | tf_op jit(solution)/shard_map/ppermute | solution.py:703
  43.1 29.3 %collective-permute-start.6 = (bf16[42,48,128]{2,1,0:T(8,128)(2,1)S(1)}, bf16[42,48,128]{2,1,0:T(8,128)(2,1)S(1)}, u32[]{:S(2)}, u32[]{:S(2)}) collective-permute-start(bf16[42,48,128]{2,1,0:T(8,128)(2,1)S(1)} %collective-permute-done.5.rest_1_.rest_8_), channel_id=1, source_target_pairs={{0,2},{2,4},{4,6},{6,8},{8,10},{10,12},{12,14},{3,1},{5,3},{7,5},{... | collective-permute-start | bytes 1548296 | tf_op jit(solution)/shard_map/ppermute | solution.py:707
  47.2 21.1 %collective-permute-start.1 = (bf16[41,48,128]{2,1,0:T(8,128)(2,1)}, bf16[41,48,128]{2,1,0:T(8,128)(2,1)}, u32[]{:S(2)}, u32[]{:S(2)}) collective-permute-start(bf16[41,48,128]{2,1,0:T(8,128)(2,1)} %get-tuple-element.65), channel_id=1, source_target_pairs={{0,1},{1,0},{2,3},{3,2},{4,5},{5,4},{6,7},{7,6},{8,9},{9,8},{10,11... | collective-permute-start | bytes 1511432 | tf_op jit(solution)/shard_map/ppermute | solution.py:685
  49.5 33.0 %collective-permute-start.7 = (bf16[41,48,128]{2,1,0:T(8,128)(2,1)}, bf16[41,48,128]{2,1,0:T(8,128)(2,1)}, u32[]{:S(2)}, u32[]{:S(2)}) collective-permute-start(bf16[41,48,128]{2,1,0:T(8,128)(2,1)} %collective-permute-done.4.rest_2_.rest_9_), channel_id=1, source_target_pairs={{0,2},{2,4},{4,6},{6,8},{8,10},{10,12},{12,14},{3,1},{5,3},{7,5},{... | collective-permute-start | bytes 1511432 | tf_op jit(solution)/shard_map/ppermute | solution.py:712
  68.2 20.5 %collective-permute-start.9 = (bf16[41,48,128]{2,1,0:T(8,128)(2,1)}, bf16[41,48,128]{2,1,0:T(8,128)(2,1)}, u32[]{:S(2)}, u32[]{:S(2)}) collective-permute-start(bf16[41,48,128]{2,1,0:T(8,128)(2,1)} %collective-permute-done.1.rest_3_.rest_10_), channel_id=1, source_target_pairs={{0,2},{2,4},{4,6},{6,8},{8,10},{10,12},{12,14},{3,1},{5,3},{7,5},{... | collective-permute-start | bytes 1511432 | tf_op jit(solution)/shard_map/ppermute | solution.py:712
  88.7 27.7 %copy-start.7 = (f32[32]{0:T(128)S(1)}, f32[32]{0:T(128)}, u32[]{:S(2)}) copy-start(f32[32]{0:T(128)} %param.21) | copy-start | bytes 388
  88.7 28.6 %copy-start.5 = (f32[512,32]{0,1:T(8,128)S(1)}, f32[512,32]{0,1:T(8,128)}, u32[]{:S(2)}) copy-start(f32[512,32]{0,1:T(8,128)} %param.17) | copy-start | bytes 196612
  91.5 16.8 %collective-permute-start.10 = (bf16[80,512]{1,0:T(8,128)(2,1)S(1)}, bf16[80,512]{1,0:T(8,128)(2,1)S(1)}, u32[]{:S(2)}, u32[]{:S(2)}) collective-permute-start(bf16[80,512]{1,0:T(8,128)(2,1)S(1)} %get-tuple-element.92), channel_id=1, source_target_pairs={{0,1},{1,0},{2,3},{3,2},{4,5},{5,4},{6,7},{7,6},{8,9},{9,8},{10,11... | collective-permute-start | bytes 245768 | tf_op jit(solution)/shard_map/ppermute | solution.py:764
  106.0 7.0 %collective-permute-start.11 = (bf16[80,512]{1,0:T(8,128)(2,1)S(1)}, bf16[80,512]{1,0:T(8,128)(2,1)S(1)}, u32[]{:S(2)}, u32[]{:S(2)}) collective-permute-start(bf16[80,512]{1,0:T(8,128)(2,1)S(1)} %get-tuple-element.93), channel_id=1, source_target_pairs={{1,2},{3,4},{5,6},{7,8},{9,10},{11,12},{13,14},{2,1},{4,3},{6,5},{... | collective-permute-start | bytes 245768 | tf_op jit(solution)/shard_map/ppermute | solution.py:766
  113.1 4.2 %collective-permute-start.12 = (f32[32,512]{1,0:T(8,128)S(1)}, f32[32,512]{1,0:T(8,128)S(1)}, u32[]{:S(2)}, u32[]{:S(2)}) collective-permute-start(f32[32,512]{1,0:T(8,128)S(1)} %constant_dynamic-slice_fusion.1), channel_id=1, source_target_pairs={{0,16},{16,0},{1,17},{17,1},{2,18},{18,2},{3,19},{19,3},{4,20},{20... | collective-permute-start | bytes 196616 | tf_op jit(solution)/shard_map/ppermute | solution.py:775
